TPU v7x, 128 devices: a whole 4x4x4 slice. The times are simulated.
128 devices in a mesh: row: 4 (over x), col: 32 (over z, y, core).
Axes of the slice: x: 4, y: 4, z: 4, core: 2. Of those that a mesh axis runs over, the one named last changes fastest.
Arguments:
- tokens: bfloat16 [512, 8192], P('col', 'row'), may hold values from -6 to 6
- out_grad: bfloat16 [512, 8192], P('col', 'row'), may hold values from -6 to 6
- gate_weight: bfloat16 [8192, 29568], P('row', 'col'), may hold values from -0.0625 to 0.0625
- up_weight: bfloat16 [8192, 29568], P('row', 'col'), may hold values from -0.0625 to 0.0625
- down_weight: bfloat16 [29568, 8192], P('col', 'row'), may hold values from -0.03125 to 0.03125
Outputs:
- input_grad: bfloat16 [512, 8192], P('col', 'row')
- gate_wgrad: bfloat16 [8192, 29568], P('row', 'col')
- up_wgrad: bfloat16 [8192, 29568], P('row', 'col')
- down_wgrad: bfloat16 [29568, 8192], P('col', 'row')
All inputs are finite; a program needn't handle non-finite values.
Results may differ from a plain program's by a relative error of at most 0.005.
Values may be sent and summed in bfloat16 or wider, within the bound.
No kernel may reach another device: no remote copies, remote signals or barrier semaphores. Data moves between devices by JAX's collectives and lax.ppermute only.
A program may use at most 128 MiB of HBM per device.

v0:
```python
import math
import jax
import jax.numpy as jnp
from jax import lax
from jax.sharding import PartitionSpec as P


def contract(left, right, left_dim, right_dim):
    return lax.dot_general(
        left, right, (((left_dim,), (right_dim,)), ((), ())), preferred_element_type=jnp.float32
    )


def swiglu_backward(gate, upward, hid_grad):
    sig = jax.nn.sigmoid(gate)
    act = gate * sig
    hidden = (act * upward).astype(jnp.bfloat16)
    gate_grad = (hid_grad * upward * sig * (1.0 + gate * (1.0 - sig))).astype(jnp.bfloat16)
    up_grad = (hid_grad * act).astype(jnp.bfloat16)
    return (hidden, gate_grad, up_grad)


def local(tokens, out_grad, gate_weight, up_weight, down_weight):
    panel_tokens, panel_grads = (
        lax.all_gather(tokens, "col", axis=0, tiled=True),
        lax.all_gather(out_grad, "col", axis=0, tiled=True),
    )
    factor = 1.0 / math.sqrt(panel_tokens.shape[0])
    gate_part = jnp.dot(panel_tokens, gate_weight, preferred_element_type=jnp.float32)
    up_part = jnp.dot(panel_tokens, up_weight, preferred_element_type=jnp.float32)
    grad_part = contract(panel_grads, down_weight, 1, 1)
    gate, upward, hid_grad = lax.psum((gate_part, up_part, grad_part), "row")
    hidden, gate_grad, up_grad = swiglu_backward(gate, upward, hid_grad)
    input_grad = lax.psum_scatter(
        contract(gate_grad, gate_weight, 1, 1) + contract(up_grad, up_weight, 1, 1),
        "col",
        scatter_dimension=0,
        tiled=True,
    ).astype(jnp.bfloat16)
    gate_wgrad = (contract(panel_tokens, gate_grad, 0, 0) * factor).astype(jnp.bfloat16)
    up_wgrad = (contract(panel_tokens, up_grad, 0, 0) * factor).astype(jnp.bfloat16)
    down_wgrad = (contract(hidden, panel_grads, 0, 0) * factor).astype(jnp.bfloat16)
    return (input_grad, gate_wgrad, up_wgrad, down_wgrad)


def solution(mesh):
    placed = (P("col", "row"), P("col", "row"), P("row", "col"), P("row", "col"), P("col", "row"))
    return jax.shard_map(
        local,
        mesh=mesh,
        in_specs=placed,
        out_specs=(P("col", "row"), P("row", "col"), P("row", "col"), P("col", "row")),
        check_vma=False,
    )
```

profile of v0, /device:TPU:0, one launch (start us, length us, event | category | flops | bytes accessed | tf_op | source)
XLA Modules:
  0.0 326.6 jit_solution(14472059379591102396)
XLA Ops:
  7.2 0.0 all-gather.5.cloned.1.call-start
  7.2 0.7 all-gather.5.cloned.1.call-update
  7.9 0.0 all-gather.3.cloned.1.call-start
  7.9 0.7 all-gather.3.cloned.1.call-update
  8.6 0.0 all-reduce.3.cloned.1.call-start
  8.7 48.1 %all-gather.5.cloned.1.call-done = bf16[512,2048]{1,0:T(8,128)(2,1)} async-done(((bf16[16,2048]{1,0:T(8,128)(2,1)}), bf16[512,2048]{1,0:T(8,128)(2,1)}) %all-gather.5.cloned.1.call-update) | async-done | bytes 2097168 | tf_op jit(solution)/shard_map/all_gather | solution.py:25
  56.8 6.3 %fusion.6 = f32[512,924]{0,1:T(8,128)} fusion(bf16[512,2048]{1,0:T(8,128)(2,1)} %all-gather.5.cloned.1.call-done, bf16[2048,924]{0,1:T(8,128)(2,1)} %param.8), kind=kOutput, calls=%fused_computation.13 | convolution fusion | flops 1937768448 | bytes 7774208 | tf_op jit(solution)/shard_map/dot_general | solution.py:30
  63.0 0.0 copy-done
  63.0 0.0 copy-done.5
  63.0 3.4 %fusion.7 = f32[512,924]{0,1:T(8,128)} fusion(bf16[512,2048]{1,0:T(8,128)(2,1)S(1)} %copy-done.5, bf16[2048,924]{0,1:T(8,128)(2,1)S(1)} %copy-done), kind=kOutput, calls=%fused_computation.14 | convolution fusion | flops 1937768448 | bytes 7774208 | tf_op jit(solution)/shard_map/dot_general | solution.py:29
  66.4 35.8 %all-gather.3.cloned.1.call-done = bf16[512,2048]{1,0:T(8,128)(2,1)} async-done(((bf16[16,2048]{1,0:T(8,128)(2,1)}), bf16[512,2048]{1,0:T(8,128)(2,1)}) %all-gather.3.cloned.1.call-update) | async-done | bytes 2097168 | tf_op jit(solution)/shard_map/all_gather | solution.py:26
  102.3 6.1 %fusion.5 = f32[512,924]{0,1:T(8,128)} fusion(bf16[512,2048]{1,0:T(8,128)(2,1)} %all-gather.3.cloned.1.call-done, bf16[924,2048]{1,0:T(8,128)(2,1)} %param.9), kind=kOutput, calls=%fused_computation.12 | convolution fusion | flops 1937768448 | bytes 7774208 | tf_op jit(solution)/shard_map/dot_general | solution.py:9
  108.4 0.0 all-reduce.3.cloned.1.call-update
  108.4 0.2 reduce-scatter.2.cloned.1.call-start
  108.7 116.8 %all-reduce.3.cloned.1.call-done = (f32[512,924]{0,1:T(8,128)}, f32[512,924]{0,1:T(8,128)}, f32[512,924]{0,1:T(8,128)}) async-done(((f32[512,924]{0,1:T(8,128)}, f32[512,924]{0,1:T(8,128)}, f32[512,924]{0,1:T(8,128)}), (f32[512,924]{0,1:T(8,128)}, f32[512,924]{0,1:T(8,128)}, f32[512,924]{0,1:T(8,128)})) %all-reduce.3.cloned.1.call-update) | async-done | bytes 5677072 | tf_op jit(solution)/shard_map/psum | solution.py:32
  225.4 3.9 %multiply_convert_fusion.4 = (bf16[512,924]{0,1:T(8,128)(2,1)S(1)}, bf16[512,924]{0,1:T(8,128)(2,1)S(1)}) fusion(f32[512,924]{0,1:T(8,128)} %get-tuple-element.5, f32[512,924]{0,1:T(8,128)} %get-tuple-element.4, f32[512,924]{0,1:T(8,128)} %get-tuple-element.6), kind=kLoop, calls=%fused_computation.7 | loop fusion | flops 6150144 | bytes 7569408 | tf_op jit(solution)/shard_map/convert_element_type | solution.py:19
  229.3 0.0 copy-done.1
  229.3 0.0 copy-start.2
  229.3 2.4 fusion.8
  231.8 0.0 copy-done.2
  231.8 4.5 %convolution_add_fusion = f32[512,2048]{1,0:T(8,128)} fusion(f32[512,2048]{1,0:T(8,128)S(1)} %fusion.8, bf16[512,924]{0,1:T(8,128)(2,1)S(1)} %get-tuple-element.7, bf16[2048,924]{0,1:T(8,128)(2,1)S(1)} %copy-done.2), kind=kOutput, calls=%fused_computation.5 | convolution fusion | flops 1938817024 | bytes 13119488 | tf_op jit(solution)/shard_map/dot_general | solution.py:9
  236.3 0.0 reduce-scatter.2.cloned.1.call-update
  236.3 0.0 copy-start.6
  236.3 5.8 %fusion = bf16[2048,924]{0,1:T(8,128)(2,1)} fusion(bf16[512,924]{0,1:T(8,128)(2,1)S(1)} %get-tuple-element.8, bf16[512,2048]{1,0:T(8,128)(2,1)} %all-gather.5.cloned.1.call-done), kind=kOutput, calls=%fused_computation.3 | convolution fusion | flops 1941553152 | bytes 6828032 | tf_op jit(solution)/shard_map/dot_general | solution.py:9
  242.1 0.0 copy-done.6
  242.1 4.1 %fusion.1 = bf16[2048,924]{0,1:T(8,128)(2,1)} fusion(bf16[512,924]{0,1:T(8,128)(2,1)S(1)} %get-tuple-element.7, bf16[512,2048]{1,0:T(8,128)(2,1)S(1)} %copy-done.6), kind=kOutput, calls=%fused_computation.4 | convolution fusion | flops 1941553152 | bytes 6828032 | tf_op jit(solution)/shard_map/dot_general | solution.py:9
  246.2 0.0 copy-done.3
  246.2 0.0 copy-done.4
  246.2 0.0 copy-done.7
  246.2 4.1 %multiply_convert_fusion = bf16[924,2048]{1,0:T(8,128)(2,1)} fusion(bf16[512,2048]{1,0:T(8,128)(2,1)S(1)} %copy-done.7, f32[512,924]{0,1:T(8,128)S(1)} %copy-done.4, f32[512,924]{0,1:T(8,128)S(1)} %copy-done.3), kind=kOutput, calls=%fused_computation | convolution fusion | flops 1944391680 | bytes 9666560 | tf_op jit(solution)/shard_map/dot_general | solution.py:9
  250.3 68.2 %reduce-scatter.2.cloned.1.call-done = f32[16,2048]{1,0:T(8,128)} async-done(((f32[512,2048]{1,0:T(8,128)}), f32[16,2048]{1,0:T(8,128)}) %reduce-scatter.2.cloned.1.call-update) | async-done | bytes 131088 | tf_op jit(solution)/shard_map/reduce_scatter | solution.py:34
  318.5 1.5 convert_element_type.29
  (6 shorter events, 0.0 us)
Async XLA Ops:
  7.2 49.6 %all-gather.5.cloned.1.call-start = ((), (), s32[]{:S(2)}) async-start(), calls=%async_computation.2 | async-start | bytes 2162688 | tf_op jit(solution)/shard_map/all_gather | solution.py:25
  7.9 94.4 %all-gather.3.cloned.1.call-start = ((), (), s32[]{:S(2)}) async-start(), calls=%async_computation.1 | async-start | bytes 2162688 | tf_op jit(solution)/shard_map/all_gather | solution.py:26
  8.6 216.8 %all-reduce.3.cloned.1.call-start = ((), (), s32[]{:S(2)}) async-start(), calls=%async_computation.4 | async-start | bytes 11403264 | tf_op jit(solution)/shard_map/psum | solution.py:32
  56.8 6.3 %copy-start = (bf16[2048,924]{0,1:T(8,128)(2,1)S(1)}, bf16[2048,924]{0,1:T(8,128)(2,1)}, u32[]{:S(2)}) copy-start(bf16[2048,924]{0,1:T(8,128)(2,1)} %param.7) | copy-start | bytes 11354116
  56.8 6.3 %copy-start.5 = (bf16[512,2048]{1,0:T(8,128)(2,1)S(1)}, bf16[512,2048]{1,0:T(8,128)(2,1)}, u32[]{:S(2)}) copy-start(bf16[512,2048]{1,0:T(8,128)(2,1)} %all-gather.5.cloned.1.call-done) | copy-start | bytes 6291460
  108.4 210.1 %reduce-scatter.2.cloned.1.call-start = ((), (), s32[]{:S(2)}) async-start(), calls=%async_computation.3 | async-start | bytes 4325376 | tf_op jit(solution)/shard_map/reduce_scatter | solution.py:34
  225.4 3.9 %copy-start.1 = (bf16[2048,924]{0,1:T(8,128)(2,1)S(1)}, bf16[2048,924]{0,1:T(8,128)(2,1)}, u32[]{:S(2)}) copy-start(bf16[2048,924]{0,1:T(8,128)(2,1)} %param.7) | copy-start | bytes 11354116
  229.3 2.4 copy-start.2
  236.3 5.8 %copy-start.6 = (bf16[512,2048]{1,0:T(8,128)(2,1)S(1)}, bf16[512,2048]{1,0:T(8,128)(2,1)}, u32[]{:S(2)}) copy-start(bf16[512,2048]{1,0:T(8,128)(2,1)} %all-gather.5.cloned.1.call-done) | copy-start | bytes 6291460
  242.1 4.1 %copy-start.3 = (f32[512,924]{0,1:T(8,128)S(1)}, f32[512,924]{0,1:T(8,128)}, u32[]{:S(2)}) copy-start(f32[512,924]{0,1:T(8,128)} %get-tuple-element.4) | copy-start | bytes 5677060
  242.1 4.1 %copy-start.4 = (f32[512,924]{0,1:T(8,128)S(1)}, f32[512,924]{0,1:T(8,128)}, u32[]{:S(2)}) copy-start(f32[512,924]{0,1:T(8,128)} %get-tuple-element.6) | copy-start | bytes 5677060
  242.1 4.1 %copy-start.7 = (bf16[512,2048]{1,0:T(8,128)(2,1)S(1)}, bf16[512,2048]{1,0:T(8,128)(2,1)}, u32[]{:S(2)}) copy-start(bf16[512,2048]{1,0:T(8,128)(2,1)} %all-gather.3.cloned.1.call-done) | copy-start | bytes 6291460
Sparse Core Ops, SparseCore 0:
  10.3 46.4 all-gather.4
  59.0 43.2 all-gather.2
  108.5 116.8 all-reduce.2
  236.4 81.9 reduce-scatter.1
where the time goes:
time: 327 us
  waiting for transfers between devices  270 us (83%)
  matrix products  36.7 us (11%)
  between operations  13.8 us (4%)
  other arithmetic  5.43 us (2%)
    psum x1, waiting for transfers between devices, local(): gate, upward, hid_grad = lax.psum((gate_part, up_part, grad_part), 'row')  117 us
    reduce_scatter x1, waiting for transfers between devices, local(): lax.psum_scatter(contract(gate_grad, gate_weight, 1, 1) + contract(up_gra...  68.2 us
    all_gather x1, waiting for transfers between devices, local(): lax.all_gather(tokens, 'col', axis=0, tiled=True)  48.1 us
    all_gather x1, waiting for transfers between devices, local(): lax.all_gather(out_grad, 'col', axis=0, tiled=True)  35.8 us
    dot_general x6, matrix products, contract(): lax.dot_general(left, right, (((left_dim,), (right_dim,)), ((), ())), pre...  27 us
  transfers between devices with their start and end apart: 4, of which 4 were waited for; matrix products, arithmetic and copies ran while one was open for 7% of the time, Pallas kernels for 0%

commit v1 on v0

--- a/solution.py
+++ b/solution.py
@@ -3,6 +3,12 @@
 import jax.numpy as jnp
 from jax import lax
 from jax.sharding import PartitionSpec as P
+
+
+def read_bars(shard_in, lane_axis, dim_k):
+    o_now = jnp.concatenate([shard_in] * lax.axis_size(lane_axis), axis=dim_k)
+    known = lax.all_to_all(o_now, lane_axis, dim_k, dim_k, tiled=True)
+    return known
 
 
 def contract(left, right, left_dim, right_dim):
@@ -23,7 +29,7 @@
 def local(tokens, out_grad, gate_weight, up_weight, down_weight):
     panel_tokens, panel_grads = (
         lax.all_gather(tokens, "col", axis=0, tiled=True),
-        lax.all_gather(out_grad, "col", axis=0, tiled=True),
+        read_bars(out_grad, "col", 0),
     )
     factor = 1.0 / math.sqrt(panel_tokens.shape[0])
     gate_part = jnp.dot(panel_tokens, gate_weight, preferred_element_type=jnp.float32)

time: 327 us -> 294 us (0.90)
  waiting for transfers between devices: 270 us -> 185 us
  blocking collectives: 0 us -> 40 us
  local copies, waits for them, and re-layouts: 0.03 us -> 15 us
    all_gather x1, waiting for transfers between devices: 48.1 us -> 0.01 us  [local(): lax.all_gather(tokens, 'col', axis=0, tiled=True)]
    all_to_all x0 -> x1, blocking collectives: none -> 40 us  [read_bars(): known = lax.all_to_all(o_now, lane_axis, dim_k, dim_k, tiled=True)]
    all_gather x1 -> x0, waiting for transfers between devices: 35.8 us -> none  [local(): lax.all_gather(out_grad, 'col', axis=0, tiled=True)]
    unnamed x16 -> x53, local copies, waits for them, and re-layouts: 0.03 us -> 15 us
  transfers between devices with their start and end apart: 4 -> 3, of which waited for: 4 -> 2; matrix products, arithmetic and copies ran while one was open for 7% -> 11% of each run, Pallas kernels for 0% -> 0%
where the time goes in v1:
time: 294 us; the launch traced here: 293 us
  waiting for transfers between devices  185 us (63%)
  blocking collectives  40 us (14%)
  matrix products  33.9 us (12%)
  local copies, waits for them, and re-layouts  15 us (5%)
  between operations  14 us (5%)
  other arithmetic  5.43 us (2%)
    psum x1, waiting for transfers between devices, local(): gate, upward, hid_grad = lax.psum((gate_part, up_part, grad_part), 'row')  116 us
    reduce_scatter x1, waiting for transfers between devices, local(): lax.psum_scatter(contract(gate_grad, gate_weight, 1, 1) + contract(up_gra...  68.2 us
    all_to_all x1, blocking collectives, read_bars(): known = lax.all_to_all(o_now, lane_axis, dim_k, dim_k, tiled=True)  40 us
    dot_general x6, matrix products, contract(): lax.dot_general(left, right, (((left_dim,), (right_dim,)), ((), ())), pre...  24.3 us
    unnamed x53, local copies, waits for them, and re-layouts  15 us
    dot_general x1, matrix products, local(): jnp.dot(panel_tokens, up_weight, preferred_element_type=jnp.float32)  6.26 us
  transfers between devices with their start and end apart: 3, of which 2 were waited for; matrix products, arithmetic and copies ran while one was open for 11% of the time, Pallas kernels for 0%

profile of v1, /device:TPU:0, one launch (start us, length us, event | category | flops | bytes accessed | tf_op | source)
XLA Modules:
  0.0 293.3 jit_solution(10188254615536717915)
XLA Ops:
  7.2 0.7 all-gather.2.cloned.1.call-update
  8.0 0.8 constant_dynamic-update-slice_fusion.31
  8.8 0.8 constant_dynamic-update-slice_fusion.30
  9.6 0.8 constant_dynamic-update-slice_fusion.29
  10.5 0.8 constant_dynamic-update-slice_fusion.28
  11.3 0.8 constant_dynamic-update-slice_fusion.27
  12.2 0.8 constant_dynamic-update-slice_fusion.26
  13.0 0.8 constant_dynamic-update-slice_fusion.25
  13.9 0.8 constant_dynamic-update-slice_fusion.24
  14.7 0.8 constant_dynamic-update-slice_fusion.23
  15.6 0.8 constant_dynamic-update-slice_fusion.22
  16.4 0.8 constant_dynamic-update-slice_fusion.21
  17.2 0.8 constant_dynamic-update-slice_fusion.20
  18.1 0.8 constant_dynamic-update-slice_fusion.19
  18.9 0.8 constant_dynamic-update-slice_fusion.18
  19.8 0.8 constant_dynamic-update-slice_fusion.17
  20.6 0.8 constant_dynamic-update-slice_fusion.16
  21.7 40.0 %all_to_all.12 = bf16[32,16,2048]{2,1,0:T(8,128)(2,1)S(1)} all-to-all(bf16[32,16,2048]{2,1,0:T(8,128)(2,1)S(1)} %bitcast.21), channel_id=1, replica_groups=mesh['row'=4,'col'=32] {'col'}, dimensions={0} | all-to-all | bytes 4194304 | tf_op jit(solution)/shard_map/all_to_all | solution.py:10
  61.7 1.3 copy-done.4
  63.1 3.4 %fusion.5 = f32[512,924]{0,1:T(8,128)} fusion(bf16[512,2048]{1,0:T(8,128)(2,1)S(1)} %bitcast.22, bf16[924,2048]{1,0:T(8,128)(2,1)S(1)} %copy-done.8), kind=kOutput, calls=%fused_computation.44 | convolution fusion | flops 1937768448 | bytes 7774208 | tf_op jit(solution)/shard_map/dot_general | solution.py:15
  66.5 6.3 %fusion.6 = f32[512,924]{0,1:T(8,128)} fusion(bf16[512,2048]{1,0:T(8,128)(2,1)} %all-gather.2.cloned.1.call-done, bf16[2048,924]{0,1:T(8,128)(2,1)} %param.8), kind=kOutput, calls=%fused_computation.45 | convolution fusion | flops 1937768448 | bytes 7774208 | tf_op jit(solution)/shard_map/dot_general | solution.py:36
  72.7 3.4 %fusion.7 = f32[512,924]{0,1:T(8,128)} fusion(bf16[512,2048]{1,0:T(8,128)(2,1)S(1)} %copy-done.9, bf16[2048,924]{0,1:T(8,128)(2,1)S(1)} %copy-done.1), kind=kOutput, calls=%fused_computation.46 | convolution fusion | flops 1937768448 | bytes 7774208 | tf_op jit(solution)/shard_map/dot_general | solution.py:35
  76.2 0.2 reduce-scatter.2.cloned.1.call-start
  76.4 115.7 %all-reduce.3.cloned.1.call-done = (f32[512,924]{0,1:T(8,128)}, f32[512,924]{0,1:T(8,128)}, f32[512,924]{0,1:T(8,128)}) async-done(((f32[512,924]{0,1:T(8,128)}, f32[512,924]{0,1:T(8,128)}, f32[512,924]{0,1:T(8,128)}), (f32[512,924]{0,1:T(8,128)}, f32[512,924]{0,1:T(8,128)}, f32[512,924]{0,1:T(8,128)})) %all-reduce.3.cloned.1.call-update) | async-done | bytes 5677072 | tf_op jit(solution)/shard_map/psum | solution.py:38
  192.2 3.9 %multiply_convert_fusion.4 = (bf16[512,924]{0,1:T(8,128)(2,1)S(1)}, bf16[512,924]{0,1:T(8,128)(2,1)S(1)}) fusion(f32[512,924]{0,1:T(8,128)} %get-tuple-element.5, f32[512,924]{0,1:T(8,128)} %get-tuple-element.4, f32[512,924]{0,1:T(8,128)} %get-tuple-element.6), kind=kLoop, calls=%fused_computation.7 | loop fusion | flops 6150144 | bytes 7569408 | tf_op jit(solution)/shard_map/convert_element_type | solution.py:25
  196.1 2.4 fusion.8
  198.5 4.5 %convolution_add_fusion = f32[512,2048]{1,0:T(8,128)} fusion(f32[512,2048]{1,0:T(8,128)S(1)} %fusion.8, bf16[512,924]{0,1:T(8,128)(2,1)S(1)} %get-tuple-element.7, bf16[2048,924]{0,1:T(8,128)(2,1)S(1)} %copy-done.3), kind=kOutput, calls=%fused_computation.5 | convolution fusion | flops 1938817024 | bytes 13119488 | tf_op jit(solution)/shard_map/dot_general | solution.py:15
  203.1 5.8 %fusion = bf16[2048,924]{0,1:T(8,128)(2,1)} fusion(bf16[512,924]{0,1:T(8,128)(2,1)S(1)} %get-tuple-element.8, bf16[512,2048]{1,0:T(8,128)(2,1)} %all-gather.2.cloned.1.call-done), kind=kOutput, calls=%fused_computation.3 | convolution fusion | flops 1941553152 | bytes 6828032 | tf_op jit(solution)/shard_map/dot_general | solution.py:15
  208.8 4.1 %fusion.1 = bf16[2048,924]{0,1:T(8,128)(2,1)} fusion(bf16[512,924]{0,1:T(8,128)(2,1)S(1)} %get-tuple-element.7, bf16[512,2048]{1,0:T(8,128)(2,1)S(1)} %copy-done.10), kind=kOutput, calls=%fused_computation.4 | convolution fusion | flops 1941553152 | bytes 6828032 | tf_op jit(solution)/shard_map/dot_general | solution.py:15
  212.9 4.1 %multiply_convert_fusion = bf16[924,2048]{1,0:T(8,128)(2,1)} fusion(bf16[512,2048]{1,0:T(8,128)(2,1)S(1)} %bitcast.23, f32[512,924]{0,1:T(8,128)S(1)} %copy-done.7, f32[512,924]{0,1:T(8,128)S(1)} %copy-done.6), kind=kOutput, calls=%fused_computation | convolution fusion | flops 1944391680 | bytes 9666560 | tf_op jit(solution)/shard_map/dot_general | solution.py:15
  217.0 68.2 %reduce-scatter.2.cloned.1.call-done = f32[16,2048]{1,0:T(8,128)} async-done(((f32[512,2048]{1,0:T(8,128)}), f32[16,2048]{1,0:T(8,128)}) %reduce-scatter.2.cloned.1.call-update) | async-done | bytes 131088 | tf_op jit(solution)/shard_map/reduce_scatter | solution.py:40
  285.2 1.5 convert_element_type.29
  (42 shorter events, 0.3 us)
Async XLA Ops:
  7.2 14.3 %copy-start = (bf16[16,2048]{1,0:T(8,128)(2,1)S(1)}, bf16[16,2048]{1,0:T(8,128)(2,1)}, u32[]{:S(2)}) copy-start(bf16[16,2048]{1,0:T(8,128)(2,1)} %param.6) | copy-start | bytes 196612
  7.2 59.3 %all-gather.2.cloned.1.call-start = ((), (), s32[]{:S(2)}) async-start(), calls=%async_computation.2 | async-start | bytes 2162688 | tf_op jit(solution)/shard_map/all_gather | solution.py:31
  7.9 184.2 %all-reduce.3.cloned.1.call-start = ((), (), s32[]{:S(2)}) async-start(), calls=%async_computation.4 | async-start | bytes 11403264 | tf_op jit(solution)/shard_map/psum | solution.py:38
  21.7 41.4 %copy-start.8 = (bf16[924,2048]{1,0:T(8,128)(2,1)S(1)}, bf16[924,2048]{1,0:T(8,128)(2,1)}, u32[]{:S(2)}) copy-start(bf16[924,2048]{1,0:T(8,128)(2,1)} %param.9) | copy-start | bytes 11354116
  61.7 1.3 copy-start.4
  66.5 6.3 %copy-start.1 = (bf16[2048,924]{0,1:T(8,128)(2,1)S(1)}, bf16[2048,924]{0,1:T(8,128)(2,1)}, u32[]{:S(2)}) copy-start(bf16[2048,924]{0,1:T(8,128)(2,1)} %param.7) | copy-start | bytes 11354116
  66.5 6.3 %copy-start.9 = (bf16[512,2048]{1,0:T(8,128)(2,1)S(1)}, bf16[512,2048]{1,0:T(8,128)(2,1)}, u32[]{:S(2)}) copy-start(bf16[512,2048]{1,0:T(8,128)(2,1)} %all-gather.2.cloned.1.call-done) | copy-start | bytes 6291460
  76.2 209.0 %reduce-scatter.2.cloned.1.call-start = ((), (), s32[]{:S(2)}) async-start(), calls=%async_computation.3 | async-start | bytes 4325376 | tf_op jit(solution)/shard_map/reduce_scatter | solution.py:40
  192.2 3.9 %copy-start.2 = (bf16[2048,924]{0,1:T(8,128)(2,1)S(1)}, bf16[2048,924]{0,1:T(8,128)(2,1)}, u32[]{:S(2)}) copy-start(bf16[2048,924]{0,1:T(8,128)(2,1)} %param.7) | copy-start | bytes 11354116
  196.1 2.4 copy-start.3
  203.1 5.8 %copy-start.10 = (bf16[512,2048]{1,0:T(8,128)(2,1)S(1)}, bf16[512,2048]{1,0:T(8,128)(2,1)}, u32[]{:S(2)}) copy-start(bf16[512,2048]{1,0:T(8,128)(2,1)} %all-gather.2.cloned.1.call-done) | copy-start | bytes 6291460
  208.8 4.1 %copy-start.5 = (bf16[32,16,2048]{2,1,0:T(8,128)(2,1)S(1)}, bf16[32,16,2048]{2,1,0:T(8,128)(2,1)}, u32[]{:S(2)}) copy-start(bf16[32,16,2048]{2,1,0:T(8,128)(2,1)} %copy-done.4) | copy-start | bytes 6291460
  208.8 4.1 %copy-start.6 = (f32[512,924]{0,1:T(8,128)S(1)}, f32[512,924]{0,1:T(8,128)}, u32[]{:S(2)}) copy-start(f32[512,924]{0,1:T(8,128)} %get-tuple-element.4) | copy-start | bytes 5677060
  208.8 4.1 %copy-start.7 = (f32[512,924]{0,1:T(8,128)S(1)}, f32[512,924]{0,1:T(8,128)}, u32[]{:S(2)}) copy-start(f32[512,924]{0,1:T(8,128)} %get-tuple-element.6) | copy-start | bytes 5677060
Sparse Core Ops, SparseCore 0:
  10.3 55.3 all-gather.1
  76.3 115.8 all-reduce.2
  203.2 81.9 reduce-scatter.1
